TPU v7x, 512 devices: a whole 4x4x16 slice. The times are simulated.
512 devices in a mesh: virt: 32 (over y_lo, z), ao: 16 (over y_hi, x, core).
Axes of the slice: x: 4, y: 4 (y_hi: 2, y_lo: 2; y = y_hi * 2 + y_lo), z: 16, core: 2. Of those that a mesh axis runs over, the one named last changes fastest.
Arguments:
- density: bfloat16 [640, 640, 128], P('virt', 'ao'), may hold values from -6 to 6
- virt_coeff: bfloat16 [640, 1024], P('virt'), may hold values from -0.25 to 0.25
- block_coeff: bfloat16 [128, 1024], P('ao'), may hold values from -0.5 to 0.5
- ao_order: int32 [1024], replicated, may hold values from 0 to 1023, each once
Outputs:
- density_ao: bfloat16 [1024, 1024, 1024], P('ao', 'virt')
Inputs may be any that keep to these rules, and one draw needn't show every extreme that they name: `ao_order`: each basis function appears exactly once.
All inputs are finite; a program needn't handle non-finite values.
Results may differ from a plain program's by a relative error of at most 0.0057.
Values may be sent and summed in bfloat16 or wider, within the bound.
A program may use at most 64 MiB of HBM per device.

v0:
```python
import jax
import jax.numpy as jnp
from jax import lax
from jax.experimental import pallas as pl
from jax.experimental.pallas import tpu as pltpu
from jax.sharding import PartitionSpec as P

MESH = pl.DeviceIdType.MESH
BF = jnp.bfloat16
F32 = jnp.float32
TN = (((0,), (0,)), ((), ()))
NT = (((1,), (1,)), ((), ()))
STEPS = 4
BLOCKS = [(y % 2, (y // 2) * 8 + x * 2 + c) for c in range(2) for x in range(4) for y in range(4)]
BLOCKS += [(y % 2, 16 + (y // 2) * 2 + h) for h in range(2) for y in range(4)]


def exchange(
    order_hbm, d_ref, c_ref, b_ref, o_ref,
    order, dl, cl, bl, hot, pt, kp, df, dp, cf, cp, tt, s, r, rf, g, gh, tm, tq, hb, ho, hq,
    order_sem, ds, dr, des, der, dks, dkr, bs, br, bks, bkr, zcs, zcr, ycs, ycr, xcs, xcr, fcs, fcr, kcs, kcr,
    zs, zr, ys, yr, xs, xr, fs, fr, hs, hr, yhs, yhr, xhs, xhr, fhs, fhr, qs, qr,
):
    v, j = lax.axis_index("virt"), lax.axis_index("ao")
    y_lo, z = v // 16, v % 16
    core, x, y_hi = j % 2, (j // 2) % 4, j // 8
    y = 2 * y_hi + y_lo
    share = j % 4
    right, left, far = (x + 1) % 4, (x + 3) % 4, (x + 2) % 4
    chip = j // 2

    def lanes_of(yh, e):
        return pl.ds(pl.multiple_of(yh * 512 + core * 256 + e * 128, 128), 128)

    lanes = lanes_of(x // 2, x % 2)

    def dev(yy, xx):
        return (yy % 2) * 16 + z, (yy // 2) * 8 + xx * 2 + core

    other = (v, j + 1 - 2 * core)
    to_right, to_left = dev(y, right), dev(y, left)

    def remote(src, dst, send, recv, device):
        return pltpu.make_async_remote_copy(
            src_ref=src, dst_ref=dst, send_sem=send, recv_sem=recv, device_id=device, device_id_type=MESH
        )

    def arrived(ref, sem):
        remote(ref, ref, sem, sem, other).wait_recv()

    def left_for(ref, sem):
        remote(ref, ref, sem, sem, other).wait_send()

    order_copy = pltpu.make_async_copy(order_hbm, order, order_sem)
    order_copy.start()

    barrier = pltpu.get_barrier_semaphore()
    for dy in (1, 3):
        pl.semaphore_signal(barrier, inc=1, device_id=dev((y + dy) % 4, x), device_id_type=MESH)

    pl.semaphore_signal(barrier, inc=1, device_id=other, device_id_type=MESH)

    @pl.loop(1, 8)
    def _(t):
        pl.semaphore_signal(barrier, inc=1, device_id=(v, (j + 2 * t) % 16), device_id_type=MESH)

    @pl.loop(1, 16)
    def _(t):
        zv = y_lo * 16 + (z + t) % 16
        pl.semaphore_signal(barrier, inc=1, device_id=(zv, j), device_id_type=MESH)

        @pl.when(z // 8 != core)
        def _():
            pl.semaphore_signal(barrier, inc=1, device_id=(zv, j + 1 - 2 * core), device_id_type=MESH)

    pl.semaphore_wait(barrier, 32 + (z // 8 + core) % 2)

    @pl.loop(1, 16)
    def _(t):
        remote(c_ref.at[:, lanes], cl.at[x, y_lo, z], zcs.at[t], zcr, (y_lo * 16 + (z + t) % 16, j)).start()

    pltpu.make_async_copy(c_ref.at[:, lanes], cl.at[x, y_lo, z], zcr).start()

    @pl.loop(1, 8)
    def _(t):
        jj = (j + 2 * t) % 16
        remote(d_ref.at[pl.ds(jj // 2 * 2, 2)], dl.at[pl.ds(0, 2), core, chip], ds, dr, (v, jj)).start()
        remote(d_ref.at[16 + jj // 4], dl.at[2, core, chip], des, der, (v, jj)).start()

    pltpu.make_async_copy(d_ref.at[pl.ds(chip * 2, 2)], dl.at[pl.ds(0, 2), core, chip], dr).start()
    pltpu.make_async_copy(d_ref.at[16 + j // 4], dl.at[2, core, chip], der).start()

    order_copy.wait()
    column = lax.broadcasted_iota(jnp.int32, (1, 1024), 1)

    @pl.loop(0, 128)
    def _(k):
        hot[pl.ds(k, 1), :] = jnp.where(column == order[chip * 128 + k], 1.0, 0.0).astype(F32)

    def coeff_x(part, yl):
        blk = cl.at[x, yl]
        remote(blk, blk, xcs.at[0, part], xcr.at[0, part], to_right).start()
        remote(blk, blk, xcs.at[1, part], xcr.at[1, part], to_left).start()

    def coeff_on(part, yl):
        for way, (frm, device) in enumerate(((left, to_right), (right, to_left))):
            arrived(cl.at[frm, yl], xcr.at[way, part])
            blk = cl.at[frm, yl, pl.ds(way * 8, 8)]
            remote(blk, blk, fcs.at[way, part], fcr.at[way, part], device).start()

    arrived(cl.at[x, y_lo], zcr)
    for e, dy in enumerate((3, 1)):
        blk = cl.at[x, y_lo, pl.ds(e * 8, 8)]
        remote(blk, blk, ycs.at[e], ycr, dev((y + dy) % 4, x)).start()
    coeff_x(0, y_lo)

    arrived(dl.at[pl.ds(0, 2), core], dr)
    arrived(dl.at[2, core], der)
    remote(dl.at[:, core], dl.at[:, core], dks, dkr, other).start()

    arrived(cl.at[x, 1 - y_lo], ycr)
    coeff_x(1, 1 - y_lo)
    coeff_on(0, y_lo)

    arrived(dl.at[:, 1 - core], dkr)
    for u in range(3):
        for jj in range(16):
            df[u, pl.ds(jj * 40, 40), :] = dl[u, jj % 2, jj // 2].astype(F32)
        for q, (yl, i) in enumerate(BLOCKS):
            dp[pl.ds(q * 16, 16), pl.ds(u * 128, 128)] = df[u, pl.ds(yl * 320 + i, 16, stride=20), :].astype(BF)

    coeff_on(1, 1 - y_lo)

    @pl.loop(1, 8)
    def _(t):
        remote(b_ref, bl.at[core, chip], bs, br, (v, (j + 2 * t) % 16)).start()

    pltpu.make_async_copy(b_ref, bl.at[core, chip], br).start()

    def both_ways(blocks, send, recv):
        for half in range(2):
            for way, device in enumerate((to_right, to_left)):
                blk = blocks(half ^ way)
                remote(blk, blk, send.at[way, half], recv.at[way, half], device).start()

    def relay(xx):
        for yl in range(2):
            for zz in range(16):
                cf[yl * 16 + zz, pl.ds(0, 20), :] = cl[xx, yl, zz].astype(F32)
        flat = cf.reshape(32 * 24, 128)
        to = lanes_of(xx // 2, xx % 2)
        for q, (yl, i) in enumerate(BLOCKS):
            cp[pl.ds(q * 16, 16), to] = flat[pl.ds(yl * 384 + i, 16, stride=24), :].astype(BF)
        tt[xx] = lax.dot_general(cp[:, to], dp[...], TN, preferred_element_type=F32).astype(BF)

    relay(x)
    relay(left)
    relay(right)
    for way in range(2):
        arrived(cl.at[far, y_lo, pl.ds(way * 8, 8)], fcr.at[way, 0])
        arrived(cl.at[far, 1 - y_lo, pl.ds(way * 8, 8)], fcr.at[way, 1])
    relay(far)

    def regroup(k):
        for yh in range(2):
            for e in range(2):
                for q in range(4):
                    rows = tt[2 * yh + e, q * 32 + k * 8:q * 32 + k * 8 + 8, :]
                    s[0, k, e * 4 + q, pl.ds(yh * 8, 8), :] = rows[:, :128]
                    s[1, k, e * 4 + q, pl.ds(yh * 8, 8), :] = rows[:, 128:256]
                    s[k % 2, k, e * 4 + q, pl.ds(16 + yh * 8, 8), :] = rows[:, 256:]

    def whole(k, c):
        return jnp.logical_and(c == k % 2, x % 2 == k // 2)

    def to_planes(k):
        for c in range(2):
            def along_z(part):
                @pl.loop(0, 8)
                def _(w):
                    zl = (z + w) % 8
                    zz = core * 8 + zl
                    itself = jnp.logical_and(zz == z, c == core)

                    @pl.when(itself)
                    def _():
                        pltpu.make_async_copy(s.at[c, k, zl, part], r.at[k, z, part], zr.at[k]).start()

                    @pl.when(jnp.logical_not(itself))
                    def _():
                        remote(s.at[c, k, zl, part], r.at[k, z, part], zs.at[k, c], zr.at[k],
                               (y_lo * 16 + zz, chip * 2 + c)).start()

            @pl.when(whole(k, c))
            def _():
                along_z(pl.ds(0, 32))

            @pl.when(jnp.logical_not(whole(k, c)))
            def _():
                along_z(pl.ds(0, 16))

    def at(block, count=1):
        return pl.ds(pl.multiple_of(block * 16, 16), count * 16)

    def piece(k):
        return pl.ds(k * 8, 8)

    def turn(k, first, dst):
        for zz in range(16):
            rf[pl.ds(zz * 16, 16), :] = r[k, zz, pl.ds(first, 16), :].astype(F32)
        for i in range(16):
            dst[i // 8, i % 8] = rf[pl.ds(i, 16, stride=16), :].astype(BF)

    def main(k, xx, first=0, count=4):
        return tm.at[piece(k), at(xx * 4 + first, count), :]

    def pooled(k, xx, first=0, count=4):
        return tq.at[piece(k), at((xx // 2) * 4 + first, count), :]

    def along_y(k):
        @pl.when(share != k)
        def _():
            arrived(r.at[k, :, pl.ds(0, 16)], zr.at[k])

        @pl.when(share == k)
        def _():
            arrived(r.at[k], zr.at[k])

        turn(k, 0, g.at[k])
        for dy in (1, 3, 2):
            half = y_lo if dy == 2 else 1 - y_lo
            remote(g.at[k, half], main(k, x, y, 1), ys.at[k], yr.at[k], dev((y + dy) % 4, x)).start()
        tm[piece(k), at(x * 4 + y), :] = g[k, y_lo]

        @pl.when(share == k)
        def _():
            turn(k, 16, gh)
            for dy in (1, 3, 2):
                half = y_lo if dy == 2 else 1 - y_lo
                remote(gh.at[half], pooled(k, x, y, 1), yhs, yhr, dev((y + dy) % 4, x)).start()
            tq[piece(k), at((x // 2) * 4 + y), :] = gh[y_lo]

    def along_x(k):
        arrived(main(k, x, 0, 3), yr.at[k])
        both_ways(lambda part: main(k, x, 2 * part, 2), xs.at[k], xr.at[k])

        @pl.when(share == k)
        def _():
            arrived(pooled(k, x, 0, 3), yhr)
            both_ways(lambda part: pooled(k, x, 2 * part, 2), xhs, xhr)

    def between(k):
        return jnp.logical_and(core == k % 2, x % 2 != k // 2)

    def pass_on(k):
        for way, (frm, device) in enumerate(((left, to_right), (right, to_left))):
            blk = main(k, frm, 2 * way, 2)
            arrived(blk, xr.at[k, way, 0])
            remote(blk, blk, fs.at[k, way], fr.at[k, way], device).start()

        @pl.when(between(k))
        def _():
            for way, (frm, device) in enumerate(((left, to_right), (right, to_left))):
                blk = pooled(k, frm, 2 * way, 2)
                arrived(blk, xhr.at[way, 0])
                remote(blk, blk, fhs.at[way], fhr.at[way], device).start()

    def sides(k):
        for way, frm in enumerate((left, right)):
            arrived(main(k, frm, 2 - 2 * way, 2), xr.at[k, way, 1])

        @pl.when(between(k))
        def _():
            for way, frm in enumerate((left, right)):
                arrived(pooled(k, frm, 2 - 2 * way, 2), xhr.at[way, 1])

    mine_at = pl.ds(pl.multiple_of(core * 256, 256), 256)
    theirs_at = pl.ds(pl.multiple_of((1 - core) * 256, 256), 256)
    pool_at = pl.ds(512, 128)

    def to_s(k):
        arrived(main(k, far, 0, 2), fr.at[k, 0])
        arrived(main(k, far, 2, 2), fr.at[k, 1])
        terms = jnp.concatenate([tm[k * 8 + n] for n in range(8)], axis=1)
        ho[k] = lax.dot_general(kp[1 - core], terms, NT, preferred_element_type=F32).astype(BF)
        remote(ho.at[k], hb.at[k, :, mine_at], hs.at[k], hr.at[k], other).start()

        @pl.when(core == k % 2)
        def _():
            @pl.when(share == k)
            def _():
                arrived(pooled(k, far, 0, 2), fhr.at[0])
                arrived(pooled(k, far, 2, 2), fhr.at[1])

            terms = jnp.concatenate([tq[k * 8 + n] for n in range(8)], axis=1)
            hq[k] = lax.dot_general(kp[1 - core], terms, NT, preferred_element_type=F32).astype(BF)
            remote(hq.at[k], hb.at[k, :, pool_at], qs.at[k], qr.at[k], other).start()
            hb[k, :, pool_at] = lax.dot_general(kp[core], terms, NT, preferred_element_type=F32).astype(BF)

        terms = jnp.concatenate([tm[k * 8 + n] for n in range(8)], axis=1)
        hb[k, :, mine_at] = lax.dot_general(kp[core], terms, NT, preferred_element_type=F32).astype(BF)

    def to_m(k):
        arrived(hb.at[k, :, theirs_at], hr.at[k])

        @pl.when(core != k % 2)
        def _():
            arrived(hb.at[k, :, pool_at], qr.at[k])

        @pl.loop(0, 4)
        def _(q):
            cols = pl.ds(pl.multiple_of(q * 256, 256), 256)
            out = jnp.dot(hb[k], cp[:, cols], preferred_element_type=F32)
            o_ref[:, pl.ds(k * 8, 8), cols] = out.reshape(64, 8, 256).astype(BF)

    for k in range(3):
        regroup(k)
        to_planes(k)
    along_y(0)
    regroup(3)
    to_planes(3)

    arrived(bl.at[core], br)
    remote(bl.at[core], bl.at[core], bks, bkr, other).start()
    arrived(bl.at[1 - core], bkr)
    block = jnp.concatenate([bl[q % 2, q // 2].astype(F32) for q in range(16)], axis=0).astype(BF)
    pt[...] = lax.dot_general(hot[...].astype(BF), block, NT, preferred_element_type=F32).astype(BF)
    spread = lax.broadcasted_iota(jnp.int32, (512, 64), 0) // 8 == lax.broadcasted_iota(jnp.int32, (512, 64), 1)
    place = lax.broadcasted_iota(jnp.int32, (512, 128), 0) % 8
    for e in range(2):
        panel = jnp.dot(jnp.where(spread, 1.0, 0.0).astype(BF), pt[e * 64:(e + 1) * 64], preferred_element_type=F32)
        for n in range(8):
            kp[e, :, pl.ds(n * 128, 128)] = jnp.where(place == n, panel, 0.0).astype(BF)

    for k in range(STEPS):
        along_x(k)
        if k == 0:
            for e in range(2):
                half = cp.at[:, pl.ds(pl.multiple_of(e * 512 + core * 256, 256), 256)]
                remote(half, half, kcs.at[e], kcr.at[e], other).start()
        if k == 2:
            for e in range(2):
                arrived(cp.at[:, pl.ds(pl.multiple_of(e * 512 + (1 - core) * 256, 256), 256)], kcr.at[e])
        if k + 1 < STEPS:
            along_y(k + 1)
        if k >= 2:
            to_m(k - 2)
        if k >= 1:
            to_s(k - 1)
        pass_on(k)
        sides(k)
    to_m(STEPS - 2)
    to_s(STEPS - 1)
    to_m(STEPS - 1)

    @pl.loop(1, 16)
    def _(t):
        left_for(c_ref.at[:, lanes], zcs.at[t])

    left_for(dl.at[pl.ds(0, 2), core, pl.ds(0, 7)], ds)
    left_for(dl.at[2, core, pl.ds(0, 7)], des)
    left_for(dl.at[:, core], dks)
    left_for(bl.at[core, pl.ds(0, 7)], bs)
    left_for(bl.at[core], bks)
    for e in range(2):
        left_for(cl.at[x, y_lo, pl.ds(0, 8)], ycs.at[e])
        for half in range(2):
            left_for(cl.at[x, 0], xcs.at[e, half])
            left_for(cl.at[x, 0, pl.ds(0, 8)], fcs.at[e, half])
        left_for(cp.at[:, pl.ds(e * 256, 256)], kcs.at[e])
    left_for(main(0, x, 0, 3), yhs)
    for e in range(2):
        for half in range(2):
            left_for(main(0, x, 0, 2), xhs.at[e, half])
        left_for(main(0, x, 0, 2), fhs.at[e])
    for k in range(STEPS):
        for c in range(2):
            itself = jnp.logical_and(z // 8 == core, c == core)
            for count, few in ((7, itself), (8, jnp.logical_not(itself))):
                @pl.when(jnp.logical_and(few, whole(k, c)))
                def _():
                    left_for(s.at[c, k, pl.ds(0, count)], zs.at[k, c])

                @pl.when(jnp.logical_and(few, jnp.logical_not(whole(k, c))))
                def _():
                    left_for(s.at[c, k, pl.ds(0, count), pl.ds(0, 16)], zs.at[k, c])

        left_for(main(k, x, 0, 3), ys.at[k])
        for e in range(2):
            for half in range(2):
                left_for(main(k, x, 0, 2), xs.at[k, e, half])
            left_for(main(k, x, 0, 2), fs.at[k, e])
        left_for(ho.at[k], hs.at[k])

        @pl.when(core == k % 2)
        def _():
            left_for(hq.at[k], qs.at[k])


def shards(density, virt_coeff, block_coeff, ao_order):
    hbm = pl.BlockSpec(memory_space=pltpu.HBM)
    dma = pltpu.SemaphoreType.DMA
    one, two, four = dma, dma((2,)), dma((4,))
    return pl.pallas_call(
        exchange,
        out_shape=pltpu.VMEM((64, 32, 1024), BF),
        in_specs=[hbm] * 4,
        out_specs=pl.BlockSpec(memory_space=pltpu.VMEM),
        scratch_shapes=[
            pltpu.SMEM((1024,), jnp.int32),
            pltpu.VMEM((3, 2, 8, 40, 128), BF),
            pltpu.VMEM((4, 2, 16, 20, 128), BF),
            pltpu.VMEM((2, 8, 8, 1024), BF),
            pltpu.VMEM((128, 1024), F32),
            pltpu.VMEM((128, 128), BF),
            pltpu.VMEM((2, 512, 1024), BF),
            pltpu.VMEM((3, 640, 128), F32),
            pltpu.VMEM((640, 384), BF),
            pltpu.VMEM((32, 24, 128), F32),
            pltpu.VMEM((640, 1024), BF),
            pltpu.VMEM((4, 128, 384), BF),
            pltpu.VMEM((2, STEPS, 8, 32, 128), BF),
            pltpu.VMEM((STEPS, 16, 32, 128), BF),
            pltpu.VMEM((256, 128), F32),
            pltpu.VMEM((STEPS, 2, 8, 16, 128), BF),
            pltpu.VMEM((2, 8, 16, 128), BF),
            pltpu.VMEM((32, 256, 128), BF),
            pltpu.VMEM((32, 128, 128), BF),
            pltpu.VMEM((STEPS, 512, 640), BF),
            pltpu.VMEM((STEPS, 512, 256), BF),
            pltpu.VMEM((STEPS, 512, 128), BF),
            one,
            one, one, one, one, one, one,
            one, one, one, one,
            dma((16,)), one, two, one, dma((2, 2)), dma((2, 2)), dma((2, 2)), dma((2, 2)), two, two,
            dma((4, 2)), four, four, four, dma((4, 2, 2)), dma((4, 2, 2)), dma((4, 2)), dma((4, 2)), four, four,
            one, one, dma((2, 2)), dma((2, 2)), two, two, four, four,
        ],
        compiler_params=pltpu.CompilerParams(
            collective_id=0, has_side_effects=True, vmem_limit_bytes=56 * 1024 * 1024
        ),
    )(ao_order, density, virt_coeff, block_coeff)


def solution(mesh):
    return jax.shard_map(
        shards,
        mesh=mesh,
        in_specs=(P("virt", "ao", None), P("virt", None), P("ao", None), P()),
        out_specs=P("ao", "virt", None),
        check_vma=False,
    )
```

profile of v0, /device:TPU:33, one launch (start us, length us, event | category | flops | bytes accessed | tf_op | source)
XLA Modules:
  0.0 92.6 jit_solution(2502814647204153167)
XLA Ops:
  0.0 90.5 %shard_map.46 = bf16[64,32,1024]{2,1,0:T(8,128)(2,1)S(1)} custom-call(s32[1024]{0:T(1024)} %order_hbm.1, bf16[20,40,128]{2,1,0:T(8,128)(2,1)} %d_ref.1, bf16[20,1024]{1,0:T(8,128)(2,1)} %c_ref.1, bf16[8,1024]{1,0:T(8,128)(2,1)} %b_ref.1), custom_call_target="tpu_custom_call" | custom-call | tf_op jit(solution)/shard_map/pallas_call | solution.py:404
  90.5 2.0 %copy.6 = bf16[64,32,1024]{2,1,0:T(8,128)(2,1)} copy(bf16[64,32,1024]{2,1,0:T(8,128)(2,1)S(1)} %shard_map.46) | data formatting | bytes 8388608
where the time goes:
time: 92.7 us; the launch traced here: 92.6 us
  Pallas kernels  90.5 us (98%)
  local copies, waits for them, and re-layouts  2.02 us (2%)
    pallas_call x1, Pallas kernels, shards(): pl.pallas_call(exchange, out_shape=pltpu.VMEM((64, 32, 1024), BF), in_spe...  90.5 us
    unnamed x1, local copies, waits for them, and re-layouts  2.02 us

commit v1 on v0

--- a/solution.py
+++ b/solution.py
@@ -17,7 +17,7 @@
 
 def exchange(
     order_hbm, d_ref, c_ref, b_ref, o_ref,
-    order, dl, cl, bl, hot, pt, kp, df, dp, cf, cp, tt, s, r, rf, g, gh, tm, tq, hb, ho, hq,
+    order, dl, cl, bl, hot, pt, kp, df, dp, cf, cp, tt, s, r, rf, g, gh, gx, tm, tq, hb, ho, hq,
     order_sem, ds, dr, des, der, dks, dkr, bs, br, bks, bkr, zcs, zcr, ycs, ycr, xcs, xcr, fcs, fcr, kcs, kcr,
     zs, zr, ys, yr, xs, xr, fs, fr, hs, hr, yhs, yhr, xhs, xhr, fhs, fhr, qs, qr,
 ):
@@ -55,6 +55,19 @@
     order_copy.start()
 
     barrier = pltpu.get_barrier_semaphore()
+
+    def to_and_fro(w):
+        return (w + 1) // 2 * (1 - 2 * (w % 2))
+
+    @pl.loop(0, 15)
+    def _(w):
+        zv = y_lo * 16 + (z + 8 + to_and_fro(w)) % 16
+        pl.semaphore_signal(barrier, inc=1, device_id=(zv, j), device_id_type=MESH)
+
+        @pl.when(z // 8 != core)
+        def _():
+            pl.semaphore_signal(barrier, inc=1, device_id=(zv, j + 1 - 2 * core), device_id_type=MESH)
+
     for dy in (1, 3):
         pl.semaphore_signal(barrier, inc=1, device_id=dev((y + dy) % 4, x), device_id_type=MESH)
 
@@ -64,20 +77,12 @@
     def _(t):
         pl.semaphore_signal(barrier, inc=1, device_id=(v, (j + 2 * t) % 16), device_id_type=MESH)
 
-    @pl.loop(1, 16)
-    def _(t):
-        zv = y_lo * 16 + (z + t) % 16
-        pl.semaphore_signal(barrier, inc=1, device_id=(zv, j), device_id_type=MESH)
-
-        @pl.when(z // 8 != core)
-        def _():
-            pl.semaphore_signal(barrier, inc=1, device_id=(zv, j + 1 - 2 * core), device_id_type=MESH)
-
     pl.semaphore_wait(barrier, 32 + (z // 8 + core) % 2)
 
-    @pl.loop(1, 16)
-    def _(t):
-        remote(c_ref.at[:, lanes], cl.at[x, y_lo, z], zcs.at[t], zcr, (y_lo * 16 + (z + t) % 16, j)).start()
+    @pl.loop(0, 15)
+    def _(w):
+        zv = y_lo * 16 + (z + 8 + to_and_fro(w)) % 16
+        remote(c_ref.at[:, lanes], cl.at[x, y_lo, z], zcs.at[w], zcr, (zv, j)).start()
 
     pltpu.make_async_copy(c_ref.at[:, lanes], cl.at[x, y_lo, z], zcr).start()
 
@@ -173,12 +178,14 @@
     def whole(k, c):
         return jnp.logical_and(c == k % 2, x % 2 == k // 2)
 
+    start = 8 + 4 * (1 - (z // 8 + core) % 2)
+
     def to_planes(k):
         for c in range(2):
             def along_z(part):
                 @pl.loop(0, 8)
                 def _(w):
-                    zl = (z + w) % 8
+                    zl = (z + start + to_and_fro(w)) % 8
                     zz = core * 8 + zl
                     itself = jnp.logical_and(zz == z, c == core)
 
@@ -214,8 +221,8 @@
     def main(k, xx, first=0, count=4):
         return tm.at[piece(k), at(xx * 4 + first, count), :]
 
-    def pooled(k, xx, first=0, count=4):
-        return tq.at[piece(k), at((xx // 2) * 4 + first, count), :]
+    def pooled(k, xx):
+        return gx.at[k // 2, :, :, xx // 2]
 
     def along_y(k):
         @pl.when(share != k)
@@ -235,22 +242,20 @@
         @pl.when(share == k)
         def _():
             turn(k, 16, gh)
-            for dy in (1, 3, 2):
-                half = y_lo if dy == 2 else 1 - y_lo
-                remote(gh.at[half], pooled(k, x, y, 1), yhs, yhr, dev((y + dy) % 4, x)).start()
-            tq[piece(k), at((x // 2) * 4 + y), :] = gh[y_lo]
+            gx[k // 2, :, :, x // 2] = gh[...]
+            for way, device in enumerate((to_right, to_left)):
+                remote(pooled(k, x), pooled(k, x), xhs.at[way], xhr.at[way], device).start()
 
     def along_x(k):
         arrived(main(k, x, 0, 3), yr.at[k])
         both_ways(lambda part: main(k, x, 2 * part, 2), xs.at[k], xr.at[k])
 
-        @pl.when(share == k)
-        def _():
-            arrived(pooled(k, x, 0, 3), yhr)
-            both_ways(lambda part: pooled(k, x, 2 * part, 2), xhs, xhr)
-
-    def between(k):
-        return jnp.logical_and(core == k % 2, x % 2 != k // 2)
+        @pl.when(jnp.logical_and(core == k % 2, x % 2 != k // 2))
+        def _():
+            for way, (frm, device) in enumerate(((left, to_right), (right, to_left))):
+                arrived(pooled(k, frm), xhr.at[way])
+                blk = gx.at[k // 2, way, :, frm // 2]
+                remote(blk, blk, fhs.at[way], fhr.at[way], device).start()
 
     def pass_on(k):
         for way, (frm, device) in enumerate(((left, to_right), (right, to_left))):
@@ -258,21 +263,21 @@
             arrived(blk, xr.at[k, way, 0])
             remote(blk, blk, fs.at[k, way], fr.at[k, way], device).start()
 
-        @pl.when(between(k))
-        def _():
-            for way, (frm, device) in enumerate(((left, to_right), (right, to_left))):
-                blk = pooled(k, frm, 2 * way, 2)
-                arrived(blk, xhr.at[way, 0])
-                remote(blk, blk, fhs.at[way], fhr.at[way], device).start()
+        @pl.when(core == k % 2)
+        def _():
+            @pl.when(share == k)
+            def _():
+                for way in range(2):
+                    arrived(gx.at[k // 2, way, :, far // 2], fhr.at[way])
+
+            for dy in (1, 3, 2):
+                half = y_lo if dy == 2 else 1 - y_lo
+                remote(gx.at[k // 2, half], tq.at[piece(k), :, y], yhs.at[k // 2], yhr.at[k // 2], dev((y + dy) % 4, x)).start()
+            tq[piece(k), :, y] = gx[k // 2, y_lo]
 
     def sides(k):
         for way, frm in enumerate((left, right)):
             arrived(main(k, frm, 2 - 2 * way, 2), xr.at[k, way, 1])
-
-        @pl.when(between(k))
-        def _():
-            for way, frm in enumerate((left, right)):
-                arrived(pooled(k, frm, 2 - 2 * way, 2), xhr.at[way, 1])
 
     mine_at = pl.ds(pl.multiple_of(core * 256, 256), 256)
     theirs_at = pl.ds(pl.multiple_of((1 - core) * 256, 256), 256)
@@ -287,12 +292,8 @@
 
         @pl.when(core == k % 2)
         def _():
-            @pl.when(share == k)
-            def _():
-                arrived(pooled(k, far, 0, 2), fhr.at[0])
-                arrived(pooled(k, far, 2, 2), fhr.at[1])
-
-            terms = jnp.concatenate([tq[k * 8 + n] for n in range(8)], axis=1)
+            arrived(tq.at[piece(k), :, pl.ds(0, 3)], yhr.at[k // 2])
+            terms = jnp.concatenate([tq[k * 8 + n].reshape(128, 128) for n in range(8)], axis=1)
             hq[k] = lax.dot_general(kp[1 - core], terms, NT, preferred_element_type=F32).astype(BF)
             remote(hq.at[k], hb.at[k, :, pool_at], qs.at[k], qr.at[k], other).start()
             hb[k, :, pool_at] = lax.dot_general(kp[core], terms, NT, preferred_element_type=F32).astype(BF)
@@ -353,9 +354,9 @@
     to_s(STEPS - 1)
     to_m(STEPS - 1)
 
-    @pl.loop(1, 16)
-    def _(t):
-        left_for(c_ref.at[:, lanes], zcs.at[t])
+    @pl.loop(0, 15)
+    def _(w):
+        left_for(c_ref.at[:, lanes], zcs.at[w])
 
     left_for(dl.at[pl.ds(0, 2), core, pl.ds(0, 7)], ds)
     left_for(dl.at[2, core, pl.ds(0, 7)], des)
@@ -368,11 +369,10 @@
             left_for(cl.at[x, 0], xcs.at[e, half])
             left_for(cl.at[x, 0, pl.ds(0, 8)], fcs.at[e, half])
         left_for(cp.at[:, pl.ds(e * 256, 256)], kcs.at[e])
-    left_for(main(0, x, 0, 3), yhs)
     for e in range(2):
-        for half in range(2):
-            left_for(main(0, x, 0, 2), xhs.at[e, half])
-        left_for(main(0, x, 0, 2), fhs.at[e])
+        left_for(tq.at[pl.ds(0, 8), :, pl.ds(0, 3)], yhs.at[e])
+        left_for(gx.at[0, :, :, 0], xhs.at[e])
+        left_for(gx.at[0, 0, :, 0], fhs.at[e])
     for k in range(STEPS):
         for c in range(2):
             itself = jnp.logical_and(z // 8 == core, c == core)
@@ -424,8 +424,9 @@
             pltpu.VMEM((256, 128), F32),
             pltpu.VMEM((STEPS, 2, 8, 16, 128), BF),
             pltpu.VMEM((2, 8, 16, 128), BF),
+            pltpu.VMEM((2, 2, 8, 2, 16, 128), BF),
             pltpu.VMEM((32, 256, 128), BF),
-            pltpu.VMEM((32, 128, 128), BF),
+            pltpu.VMEM((32, 2, 4, 16, 128), BF),
             pltpu.VMEM((STEPS, 512, 640), BF),
             pltpu.VMEM((STEPS, 512, 256), BF),
             pltpu.VMEM((STEPS, 512, 128), BF),
@@ -434,7 +435,7 @@
             one, one, one, one,
             dma((16,)), one, two, one, dma((2, 2)), dma((2, 2)), dma((2, 2)), dma((2, 2)), two, two,
             dma((4, 2)), four, four, four, dma((4, 2, 2)), dma((4, 2, 2)), dma((4, 2)), dma((4, 2)), four, four,
-            one, one, dma((2, 2)), dma((2, 2)), two, two, four, four,
+            two, two, two, two, two, two, four, four,
         ],
         compiler_params=pltpu.CompilerParams(
             collective_id=0, has_side_effects=True, vmem_limit_bytes=56 * 1024 * 1024

time: 92.7 us -> 88.2 us (0.951)
  the two profiles are of different devices: /device:TPU:33 before, /device:TPU:65 now
where the time goes in v1:
time: 88.2 us; the launch traced here: 88.1 us
  Pallas kernels  86 us (98%)
  local copies, waits for them, and re-layouts  2.02 us (2%)
    pallas_call x1, Pallas kernels, shards(): pl.pallas_call(exchange, out_shape=pltpu.VMEM((64, 32, 1024), BF), in_spe...  86 us
    unnamed x1, local copies, waits for them, and re-layouts  2.02 us

profile of v1, /device:TPU:65, one launch (start us, length us, event | category | flops | bytes accessed | tf_op | source)
XLA Modules:
  0.0 88.1 jit_solution(11738324034830202067)
XLA Ops:
  0.0 86.0 %shard_map.46 = bf16[64,32,1024]{2,1,0:T(8,128)(2,1)S(1)} custom-call(s32[1024]{0:T(1024)} %order_hbm.1, bf16[20,40,128]{2,1,0:T(8,128)(2,1)} %d_ref.1, bf16[20,1024]{1,0:T(8,128)(2,1)} %c_ref.1, bf16[8,1024]{1,0:T(8,128)(2,1)} %b_ref.1), custom_call_target="tpu_custom_call" | custom-call | tf_op jit(solution)/shard_map/pallas_call | solution.py:404
  86.1 2.0 %copy.6 = bf16[64,32,1024]{2,1,0:T(8,128)(2,1)} copy(bf16[64,32,1024]{2,1,0:T(8,128)(2,1)S(1)} %shard_map.46) | data formatting | bytes 8388608
